TPU v7x, 256 devices: a whole 4x4x8 slice. The times are simulated.
256 devices in a mesh: req: 128 (over y, z, x), patch: 2 (over core).
Axes of the slice: x: 4, y: 4, z: 8, core: 2. Of those that a mesh axis runs over, the one named last changes fastest.
Arguments:
- latents: bfloat16 [128, 8, 128, 640], P('req', 'patch'), may hold values from -6 to 6
- previous_key_values: bfloat16 [128, 1024, 1280], P('req', 'patch'), may hold values from -6 to 6
- convolution_kernel_weight: bfloat16 [5760, 640], replicated, may hold values from -0.078125 to 0.078125
- layer_norm_gain: float32 [640], replicated, may hold values from 0.25 to 1.75
- query_matrix: bfloat16 [640, 640], replicated, may hold values from -0.237170825 to 0.237170825
- key_matrix: bfloat16 [640, 640], replicated, may hold values from -10.751744 to 10.751744
- value_matrix: bfloat16 [640, 640], replicated, may hold values from -0.25 to 0.25
- output_matrix: bfloat16 [640, 640], replicated, may hold values from -0.25 to 0.25
- adapter_table: bfloat16 [128, 573440], P('req'), may hold values from -0.14941406 to 0.14941406
- request_adapter_choice: int32 [128], replicated, may hold values from 0 to 127
- parent_request: int32 [128], replicated, may hold values from 0 to 127
- adapter_bank_row: int32 [128], replicated, may hold values from 0 to 127, each once
Outputs:
- block_out: bfloat16 [128, 8, 128, 640], P('req', 'patch')
Inputs may be any that keep to these rules, and one draw needn't show every extreme that they name: `adapter_bank_row`: each bank row appears once.
All inputs are finite; a program needn't handle non-finite values.
Results may differ from a plain program's by a relative error of at most 0.0075.
Values may be sent and summed in bfloat16 or wider, within the bound.
A program may use at most 128 MiB of HBM per device.

v0:
```python
import math
import jax
import jax.numpy as jnp
from jax import lax
from jax.experimental import pallas as pl
from jax.experimental.pallas import tpu as pltpu
from jax.sharding import PartitionSpec as P

MESH = pl.DeviceIdType.MESH
F32, BF16 = jnp.float32, jnp.bfloat16
CHIPS = 128
WIDTH, ROWS, CH, RANK, HEADS = 128, 4, 640, 64, 10
POS = ROWS * WIDTH
TILE = 16 * 128
CONV, LATE = 100, 40
CONV_PLANE, LATE_PLANE, LATE_SLOT = 25, 10, 22
EARLY = ((0, 8), (8, 8), (16, 9))
PLANES = (2, 1, 3, 0)


def mm(a, b):
    return jnp.dot(a, b, preferred_element_type=F32)


def far_first(i, size):
    step = lax.div(i + 1, 2)
    return size // 2 + jnp.where(lax.rem(i, 2) == 1, -step, step)


def activate(row, window, x, zero):
    act = jax.nn.silu(x.astype(F32)).astype(BF16).astype(F32)
    if zero is not None:
        act = jnp.where(zero, 0.0, act)
    at = lax.broadcasted_iota(jnp.int32, (WIDTH, CH), 0)
    spot = pl.ds(row * WIDTH, WIDTH)
    window[spot, 0:CH] = jnp.where(at == 0, 0.0, pltpu.roll(act, 1, 0)).astype(BF16)
    window[spot, CH:2 * CH] = act.astype(BF16)
    window[spot, 2 * CH:3 * CH] = jnp.where(at == WIDTH - 1, 0.0, pltpu.roll(act, WIDTH - 1, 0)).astype(BF16)


def unfold_down(adapter, first, tiles, wide, start):
    pairs = adapter[pl.ds(first, tiles)].reshape(tiles * 16, 128).astype(F32)
    wide[pl.ds(start, tiles * 16, stride=2), :] = pairs
    wide[pl.ds(start + 1, tiles * 16, stride=2), :] = pltpu.roll(pairs, RANK, 1)


def unfold_up(adapter, first, tall, start):
    tall[start:start + 320, :] = adapter[first:first + 20].reshape(320, 128).astype(F32)
    return jnp.concatenate([tall[pl.ds(start + q, RANK, stride=5), :] for q in range(5)], axis=1).astype(BF16)


def kernel(choice_h, parent_h, bank_h, table_h, kv_h, latents_h, weight_h, gain_h, wq_h, wk_h, wv_h, wo_h, out,
           choice, parent, bank, wanted, stage, latents, weight, gain, wkqv, wo,
           source, spread, picked, late_spread, late_picked, adapter, halo,
           window, base, wide, tall, low, hidden_s, query, keys, values, mixed,
           load, spread_sem, pick_sent, pick_sem, late_spread_sem, late_pick_sem, link):
    me = lax.axis_index("req")
    core = lax.axis_index("patch")
    other = {"patch": 1 - core}
    y = lax.div(me, 32)
    column = lax.rem(me, 32)
    z, x = lax.div(column, 4), lax.rem(column, 4)

    def slot_of(plane, at):
        return lax.rem(13 * at + 9 * plane + 17 * core, 32)

    near = [lax.rem(x + 2, 4), lax.rem(x + 1, 4), lax.rem(x + 3, 4), x]

    def serve(ahead, send):
        plane = 32 * lax.rem(y + ahead, 4)

        @pl.loop(0, 7 if ahead == 0 else 8)
        def _(i):
            send(plane + 4 * lax.rem(z + far_first(i, 8), 8), near)
        if ahead == 0:
            send(plane + 4 * z, near[:3])

    slot = slot_of(y, column)
    holds = slot < CONV_PLANE
    holds_late = slot >= LATE_SLOT

    def local(source_ref, target_ref, index):
        copy = pltpu.make_async_copy(source_ref, target_ref, load.at[index])
        copy.start()
        return copy

    first = pl.multiple_of(core * (CONV * TILE), CONV * TILE)
    table_conv = local(table_h.at[:, pl.ds(first, CONV * TILE)], stage.at[:, pl.ds(0, CONV * TILE)], 0)
    first = pl.multiple_of(2 * CONV * TILE + core * (LATE * TILE), LATE * TILE)
    table_late = local(table_h.at[:, pl.ds(first, LATE * TILE)], stage.at[:, pl.ds(CONV * TILE, LATE * TILE)], 1)
    barrier = pltpu.get_barrier_semaphore()
    pl.semaphore_signal(barrier, inc=1, device_id=other, device_id_type=MESH)

    def greet(base, columns):
        for x_to in columns:
            pl.semaphore_signal(barrier, inc=1, device_id={"req": base + x_to}, device_id_type=MESH)

    for ahead in PLANES:
        serve(ahead, greet)

    ids = [local(choice_h, choice, 2), local(parent_h, parent, 3), local(bank_h, bank, 4)]
    lat_copy = local(latents_h.at[0], latents, 5)
    weight_copies = [local(weight_h.at[pl.ds(dy * 3 * CH, 3 * CH)], weight.at[pl.ds(dy * 3 * CH, 3 * CH)], 6 + dy)
                     for dy in range(3)]
    later = [local(a, b, 9 + i) for i, (a, b) in
             enumerate([(gain_h, gain), (wk_h, wkqv.at[:, pl.ds(0, CH)]), (wq_h, wkqv.at[:, pl.ds(CH, CH)]),
                        (wv_h, wkqv.at[:, pl.ds(2 * CH, CH)]), (wo_h, wo)])]

    def compact(t):
        at = pl.multiple_of(t * TILE, TILE)
        source[t] = stage[:, pl.ds(at, TILE)].astype(F32).reshape(16, 128).astype(BF16)

    def wait_tiles(count, sem):
        tiles = source.at[pl.ds(0, count)]
        pltpu.make_async_copy(tiles, tiles, sem).wait()

    def to_partner(source_ref, target_ref, index):
        copy = pltpu.make_async_remote_copy(source_ref, target_ref, link.at[2 * index], link.at[2 * index + 1],
                                            device_id=other, device_id_type=MESH)
        copy.start()
        return copy


    def compact_plane(ahead, per_plane, first_tile):
        start = first_tile + lax.rem(y + ahead, 4) * per_plane
        pl.loop(0, per_plane, unroll=5)(lambda i: compact(start + i))

    def spread_plane(ahead, first_slot, count, per_plane, first_tile, target, sem):
        plane = lax.rem(y + ahead, 4)

        def send(base, columns):
            shift = 13 * (base - 32 * plane) + 9 * plane + 17 * core
            for x_to in columns:
                s = lax.rem(shift + 13 * x_to, 32)

                @pl.when(jnp.logical_and(s >= first_slot, s < first_slot + count))
                def _():
                    pltpu.make_async_remote_copy(source.at[first_tile + plane * per_plane + s], target.at[me], sem.at[0],
                                                 sem.at[1], device_id={"req": base + x_to}, device_id_type=MESH).start()
        serve(ahead, send)

    table_conv.wait()
    compact_plane(PLANES[0], CONV_PLANE, 0)
    pl.semaphore_wait(barrier, CHIPS)
    halo_copy = to_partner(latents_h.at[0, 3 * (1 - core)], halo, 0)
    for turn in range(4):
        spread_plane(PLANES[turn], *EARLY[0], CONV_PLANE, 0, spread, spread_sem)
        if turn < 3:
            compact_plane(PLANES[turn + 1], CONV_PLANE, 0)
    for group in EARLY[1:]:
        for ahead in PLANES:
            spread_plane(ahead, *group, CONV_PLANE, 0, spread, spread_sem)
    table_late.wait()
    for ahead in PLANES:
        compact_plane(ahead, LATE_PLANE, CONV)
        spread_plane(ahead, LATE_SLOT, LATE_PLANE, LATE_PLANE, CONV - LATE_SLOT, late_spread, late_spread_sem)
    stale_keys = to_partner(kv_h.at[0, :, pl.ds(0, CH)], keys.at[pl.ds(POS, POS)], 1)
    stale_values = to_partner(kv_h.at[0, :, pl.ds(CH, CH)], values.at[pl.ds(POS, POS)], 2)

    for copy in ids:
        copy.wait()

    @pl.loop(0, CHIPS, unroll=8)
    def _(p):
        wanted[p] = bank[choice[parent[p]]]

    lat_copy.wait()
    for row in range(ROWS):
        activate(row + 1, window, latents[row], None)
    halo_copy.wait()
    activate(0, window, halo[...], core == 0)
    activate(ROWS + 1, window, halo[...], core == 1)
    base[...] = latents[...].reshape(POS, CH).astype(F32)

    def convolve(dy):
        weight_copies[dy].wait()
        base[...] += mm(window[dy * WIDTH:dy * WIDTH + POS, :], weight[dy * 3 * CH:(dy + 1) * 3 * CH, :])

    def pick_out(mine, received, chosen, tile, in_sem, sent_sem, out_sem):
        received[me] = source[mine]
        wait_tiles(CHIPS - 1, in_sem.at[1])
        adapter[tile] = received[wanted[me]]
        for ahead in PLANES:
            def send(base, columns):
                for x_to in columns:
                    chosen[base + x_to] = received[wanted[base + x_to]]
                for x_to in columns:
                    pltpu.make_async_remote_copy(chosen.at[base + x_to], adapter.at[tile], sent_sem, out_sem(ahead),
                                                 device_id={"req": base + x_to}, device_id_type=MESH).start()
            serve(ahead, send)

    def pick_conv():
        at = CONV_PLANE * y + slot
        pick_out(at, spread, picked, CONV * core + at, spread_sem, pick_sent, lambda ahead: pick_sem.at[ahead])

    pl.when(slot < EARLY[1][0])(pick_conv)
    convolve(0)
    pl.when(jnp.logical_and(holds, slot >= EARLY[1][0]))(pick_conv)

    @pl.when(holds_late)
    def _():
        at = LATE_PLANE * y + slot - LATE_SLOT
        pick_out(CONV + at, late_spread, late_picked, 2 * CONV + LATE * core + at, late_spread_sem,
                 late_pick_sem.at[0], lambda ahead: late_pick_sem.at[1])

    convolve(1)
    convolve(2)

    def wait_split(count, own, sem):
        @pl.when(own)
        def _():
            wait_tiles(count - 1, sem)

        @pl.when(jnp.logical_not(own))
        def _():
            wait_tiles(count, sem)

    forwards = []
    starts = []
    for ahead in PLANES:
        plane = lax.rem(y + 4 - ahead, 4)
        if ahead == 0:
            wait_split(CONV_PLANE, holds, pick_sem.at[ahead])
        else:
            wait_tiles(CONV_PLANE, pick_sem.at[ahead])
        at = CONV * core + CONV_PLANE * plane
        part = adapter.at[pl.ds(at, CONV_PLANE)]
        forwards.append(to_partner(part, part, 4 + ahead))
        unfold_down(adapter, at, CONV_PLANE, wide, at * 32)
        starts.append(CONV * (1 - core) + CONV_PLANE * plane)

    def low_part(part):
        if part == 0:
            got = mm(window[0:POS, :], wide[0:3 * CH, :].astype(BF16))
            return got + mm(window[WIDTH:WIDTH + POS, 0:2 * CH], wide[3 * CH:5 * CH, :].astype(BF16))
        got = mm(window[WIDTH:WIDTH + POS, 2 * CH:3 * CH], wide[5 * CH:6 * CH, :].astype(BF16))
        return got + mm(window[2 * WIDTH:2 * WIDTH + POS, :], wide[6 * CH:9 * CH, :].astype(BF16))

    @pl.when(core == 0)
    def _():
        low[...] = low_part(0)

    @pl.when(core == 1)
    def _():
        low[...] = low_part(1)

    for forward, at in zip(forwards, starts):
        forward.wait()
        unfold_down(adapter, at, CONV_PLANE, wide, at * 32)

    @pl.when(core == 0)
    def _():
        low[...] += low_part(1)

    @pl.when(core == 1)
    def _():
        low[...] += low_part(0)

    up = unfold_up(adapter, 180, tall, 0)
    hidden = (base[...] + mm(low[...][:, :RANK].astype(BF16), up)).astype(BF16)
    hidden_s[...] = hidden
    for copy in later:
        copy.wait()
    h = hidden.astype(F32)
    centred = h - jnp.mean(h, axis=-1, keepdims=True)
    var = jnp.mean(centred * centred, axis=-1, keepdims=True)
    normed = (gain[...].reshape(1, CH) * centred * lax.rsqrt(var + 1e-5)).astype(BF16)

    projected = mm(normed, wkqv[...])
    keys[0:POS, :] = projected[:, :CH].astype(BF16)
    wait_split(LATE, holds_late, late_pick_sem.at[1])
    half = adapter.at[pl.ds(2 * CONV + LATE * core, LATE)]
    late_forward = to_partner(half, half, 3)
    stale_keys.wait()
    stale_values.wait()
    late_forward.wait()
    unfold_down(adapter, 200, 20, wide, 0)
    unfold_down(adapter, 240, 20, wide, CH)
    downs = [wide[0:CH, :].astype(BF16), wide[CH:2 * CH, :].astype(BF16)]
    lows = mm(normed, jnp.concatenate(downs, axis=1)).astype(BF16)
    query[...] = (projected[:, CH:2 * CH] + mm(lows[:, :RANK], unfold_up(adapter, 220, tall, 320))).astype(BF16)
    values[0:POS, :] = (projected[:, 2 * CH:] + mm(lows[:, 128:128 + RANK], unfold_up(adapter, 260, tall, 640))).astype(BF16)

    scale = math.log2(math.e) / math.sqrt(CH // HEADS)
    block = POS // 2
    ones = jnp.ones((2 * POS, 128), BF16)
    low_lanes = lax.broadcasted_iota(jnp.int32, (block, 128), 1) < RANK

    @pl.loop(0, HEADS // 2, unroll=HEADS // 2)
    def _(pair):
        lanes = pl.ds(pl.multiple_of(pair * 128, 128), 128)
        k2 = keys[:, lanes]
        v2 = jnp.concatenate([values[:, lanes], ones], axis=1)
        for part in range(2):
            rows = pl.ds(part * block, block)
            q2 = query[rows, lanes]
            heads = []
            for side in (low_lanes, jnp.logical_not(low_lanes)):
                scores = lax.dot_general(jnp.where(side, q2, jnp.zeros_like(q2)), k2, (((1,), (1,)), ((), ())),
                                         preferred_element_type=F32)
                top = jnp.max(scores, axis=-1, keepdims=True)
                weights = jnp.exp2((scores - top) * scale).astype(BF16)
                heads.append(mm(weights, v2))
            total = jnp.where(low_lanes, heads[0][:, 128:], heads[1][:, 128:])
            mixed[rows, lanes] = (jnp.where(low_lanes, heads[0][:, :128], heads[1][:, :128]) / total).astype(BF16)

    leaving = []
    for part in range(2):
        rows, image = pl.ds(part * block, block), pl.ds(part * (ROWS // 2), ROWS // 2)
        result = hidden_s[rows, :].astype(F32) + mm(mixed[rows, :], wo[...])
        latents[image] = result.astype(BF16).reshape(ROWS // 2, WIDTH, CH)
        leaving.append(local(latents.at[image], out.at[0, image], 14 + part))

    for copy in leaving:
        copy.wait()
    wait_split(CONV, holds, spread_sem.at[0])
    wait_split(LATE, holds_late, late_spread_sem.at[0])

    @pl.when(holds)
    def _():
        wait_tiles(CHIPS - 1, pick_sent)

    @pl.when(holds_late)
    def _():
        wait_tiles(CHIPS - 1, late_pick_sem.at[0])


def body(latents, previous_key_values, convolution_kernel_weight, layer_norm_gain, query_matrix, key_matrix,
         value_matrix, output_matrix, adapter_table, request_adapter_choice, parent_request, adapter_bank_row):
    here = pl.BlockSpec(memory_space=pltpu.HBM)
    ids = pltpu.SMEM((CHIPS,), jnp.int32)
    tiles = pltpu.VMEM((CHIPS, 16, 128), BF16)
    return pl.pallas_call(
        kernel,
        out_shape=jax.ShapeDtypeStruct(latents.shape, BF16),
        in_specs=[here] * 12,
        out_specs=pl.BlockSpec(memory_space=pl.ANY),
        scratch_shapes=[
            ids, ids, ids, ids,
            pltpu.VMEM((1, (CONV + LATE) * TILE), BF16),
            pltpu.VMEM((ROWS, WIDTH, CH), BF16),
            pltpu.VMEM((9 * CH, CH), BF16),
            pltpu.VMEM((CH,), F32),
            pltpu.VMEM((CH, 3 * CH), BF16),
            pltpu.VMEM((CH, CH), BF16),
            pltpu.VMEM((CONV + LATE, 16, 128), BF16),
            tiles, tiles, tiles, tiles,
            pltpu.VMEM((2 * (CONV + LATE), 16, 128), BF16),
            pltpu.VMEM((WIDTH, CH), BF16),
            pltpu.VMEM(((ROWS + 2) * WIDTH, 3 * CH), BF16),
            pltpu.VMEM((POS, CH), F32),
            pltpu.VMEM((2 * CONV * 32, 128), F32),
            pltpu.VMEM((960, 128), F32),
            pltpu.VMEM((POS, 128), F32),
            pltpu.VMEM((POS, CH), BF16),
            pltpu.VMEM((POS, CH), BF16),
            pltpu.VMEM((2 * POS, CH), BF16),
            pltpu.VMEM((2 * POS, CH), BF16),
            pltpu.VMEM((POS, CH), BF16),
            pltpu.SemaphoreType.DMA((16,)),
            pltpu.SemaphoreType.DMA((2,)),
            pltpu.SemaphoreType.DMA,
            pltpu.SemaphoreType.DMA((4,)),
            pltpu.SemaphoreType.DMA((2,)),
            pltpu.SemaphoreType.DMA((2,)),
            pltpu.SemaphoreType.DMA((16,)),
        ],
        compiler_params=pltpu.CompilerParams(collective_id=0, has_side_effects=True, vmem_limit_bytes=44 << 20),
    )(*[pltpu.with_memory_space_constraint(a, pltpu.HBM) for a in (
        request_adapter_choice, parent_request, adapter_bank_row, adapter_table, previous_key_values, latents,
        convolution_kernel_weight, layer_norm_gain, query_matrix, key_matrix, value_matrix, output_matrix)])


def solution(mesh):
    placed = (P("req", "patch", None, None), P("req", "patch", None), P(), P(), P(), P(), P(), P(),
              P("req", None), P(), P(), P())
    return jax.shard_map(body, mesh=mesh, in_specs=placed, out_specs=P("req", "patch", None, None), check_vma=False)
```

profile of v0, /device:TPU:1, one launch (start us, length us, event | category | flops | bytes accessed | tf_op | source)
XLA Modules:
  0.0 55.1 jit_solution(9215831321130917975)
XLA Ops:
  0.0 54.2 %shard_map.118 = bf16[1,4,128,640]{3,2,1,0:T(8,128)(2,1)S(1)} custom-call(s32[128]{0:T(128)} %choice_h.1, s32[128]{0:T(128)} %parent_h.1, s32[128]{0:T(128)} %bank_h.1, bf16[1,573440]{1,0:T(2,128)(2,1)} %table_h.1, bf16[1,512,1280]{2,1,0:T(8,128)(2,1)} %kv_h.1, bf16[1,4,128,640]{3,2,1,0:T(8,128)(2,1)} %latents_h.1, bf16[5760,640]{1,0:T(8,128)(2,1)} %weight_h.1, ...), custom_call_target="tpu_custom_call" | custom-call | tf_op jit(solution)/shard_map/pallas_call | solution.py:333
  54.2 0.8 %copy.14 = bf16[1,4,128,640]{3,2,1,0:T(8,128)(2,1)} copy(bf16[1,4,128,640]{3,2,1,0:T(8,128)(2,1)S(1)} %shard_map.118) | data formatting | bytes 1310720
where the time goes:
time: 55.1 us
  Pallas kernels  54.2 us (98%)
  local copies, waits for them, and re-layouts  0.84 us (2%)
    pallas_call x1, Pallas kernels, body(): pl.pallas_call(kernel, out_shape=jax.ShapeDtypeStruct(latents.shape, BF16...  54.2 us

commit v1 on v0

--- a/solution.py
+++ b/solution.py
@@ -121,10 +121,6 @@
         return copy
 
 
-    def compact_plane(ahead, per_plane, first_tile):
-        start = first_tile + lax.rem(y + ahead, 4) * per_plane
-        pl.loop(0, per_plane, unroll=5)(lambda i: compact(start + i))
-
     def spread_plane(ahead, first_slot, count, per_plane, first_tile, target, sem):
         plane = lax.rem(y + ahead, 4)
 
@@ -140,19 +136,15 @@
         serve(ahead, send)
 
     table_conv.wait()
-    compact_plane(PLANES[0], CONV_PLANE, 0)
+    pl.loop(0, CONV, unroll=5)(compact)
+    table_late.wait()
+    pl.loop(CONV, CONV + LATE, unroll=5)(compact)
     pl.semaphore_wait(barrier, CHIPS)
     halo_copy = to_partner(latents_h.at[0, 3 * (1 - core)], halo, 0)
-    for turn in range(4):
-        spread_plane(PLANES[turn], *EARLY[0], CONV_PLANE, 0, spread, spread_sem)
-        if turn < 3:
-            compact_plane(PLANES[turn + 1], CONV_PLANE, 0)
-    for group in EARLY[1:]:
+    for group in EARLY:
         for ahead in PLANES:
             spread_plane(ahead, *group, CONV_PLANE, 0, spread, spread_sem)
-    table_late.wait()
     for ahead in PLANES:
-        compact_plane(ahead, LATE_PLANE, CONV)
         spread_plane(ahead, LATE_SLOT, LATE_PLANE, LATE_PLANE, CONV - LATE_SLOT, late_spread, late_spread_sem)
     stale_keys = to_partner(kv_h.at[0, :, pl.ds(0, CH)], keys.at[pl.ds(POS, POS)], 1)
     stale_values = to_partner(kv_h.at[0, :, pl.ds(CH, CH)], values.at[pl.ds(POS, POS)], 2)
@@ -304,15 +296,11 @@
             total = jnp.where(low_lanes, heads[0][:, 128:], heads[1][:, 128:])
             mixed[rows, lanes] = (jnp.where(low_lanes, heads[0][:, :128], heads[1][:, :128]) / total).astype(BF16)
 
-    leaving = []
     for part in range(2):
         rows, image = pl.ds(part * block, block), pl.ds(part * (ROWS // 2), ROWS // 2)
         result = hidden_s[rows, :].astype(F32) + mm(mixed[rows, :], wo[...])
-        latents[image] = result.astype(BF16).reshape(ROWS // 2, WIDTH, CH)
-        leaving.append(local(latents.at[image], out.at[0, image], 14 + part))
-
-    for copy in leaving:
-        copy.wait()
+        out[0, image] = result.astype(BF16).reshape(ROWS // 2, WIDTH, CH)
+
     wait_split(CONV, holds, spread_sem.at[0])
     wait_split(LATE, holds_late, late_spread_sem.at[0])
 
@@ -334,7 +322,7 @@
         kernel,
         out_shape=jax.ShapeDtypeStruct(latents.shape, BF16),
         in_specs=[here] * 12,
-        out_specs=pl.BlockSpec(memory_space=pl.ANY),
+        out_specs=pl.BlockSpec(memory_space=pltpu.VMEM),
         scratch_shapes=[
             ids, ids, ids, ids,
             pltpu.VMEM((1, (CONV + LATE) * TILE), BF16),
@@ -357,7 +345,7 @@
             pltpu.VMEM((2 * POS, CH), BF16),
             pltpu.VMEM((2 * POS, CH), BF16),
             pltpu.VMEM((POS, CH), BF16),
-            pltpu.SemaphoreType.DMA((16,)),
+            pltpu.SemaphoreType.DMA((14,)),
             pltpu.SemaphoreType.DMA((2,)),
             pltpu.SemaphoreType.DMA,
             pltpu.SemaphoreType.DMA((4,)),

time: 55.1 us -> 54.1 us (0.982)
  Pallas kernels: 54.2 us -> 53.1 us
    pallas_call x1, Pallas kernels: 54.2 us -> 53.1 us  [body(): pl.pallas_call(kernel, out_shape=jax.ShapeDtypeStruct(latents.shape, BF16...]
where the time goes in v1:
time: 54.1 us; the launch traced here: 54 us
  Pallas kernels  53.1 us (98%)
  local copies, waits for them, and re-layouts  0.84 us (2%)
    pallas_call x1, Pallas kernels, body(): pl.pallas_call(kernel, out_shape=jax.ShapeDtypeStruct(latents.shape, BF16...  53.1 us

profile of v1, /device:TPU:1, one launch (start us, length us, event | category | flops | bytes accessed | tf_op | source)
XLA Modules:
  0.0 54.0 jit_solution(16091958526173419213)
XLA Ops:
  0.0 53.1 %shard_map.118 = bf16[1,4,128,640]{3,2,1,0:T(8,128)(2,1)S(1)} custom-call(s32[128]{0:T(128)} %choice_h.1, s32[128]{0:T(128)} %parent_h.1, s32[128]{0:T(128)} %bank_h.1, bf16[1,573440]{1,0:T(2,128)(2,1)} %table_h.1, bf16[1,512,1280]{2,1,0:T(8,128)(2,1)} %kv_h.1, bf16[1,4,128,640]{3,2,1,0:T(8,128)(2,1)} %latents_h.1, bf16[5760,640]{1,0:T(8,128)(2,1)} %weight_h.1, ...), custom_call_target="tpu_custom_call" | custom-call | tf_op jit(solution)/shard_map/pallas_call | solution.py:321
  53.1 0.8 %copy.14 = bf16[1,4,128,640]{3,2,1,0:T(8,128)(2,1)} copy(bf16[1,4,128,640]{3,2,1,0:T(8,128)(2,1)S(1)} %shard_map.118) | data formatting | bytes 1310720
